TPU v7x, 32 devices: a whole 2x2x4 slice. The times are simulated.
32 devices in a mesh: parts: 2 (over y), span: 4 (over x, core), seq: 4 (over z).
Axes of the slice: x: 2, y: 2, z: 4, core: 2. Of those that a mesh axis runs over, the one named last changes fastest.
Arguments:
- q_in: bfloat16 [8, 1024, 4096], P(('parts', 'span'), 'seq'), parts along dimension 0, may hold values from -9 to 9
- k_in: bfloat16 [8, 1024, 4096], P(('parts', 'span'), 'seq'), parts along dimension 0, may hold values from -9 to 9
- v_in: bfloat16 [8, 1024, 4096], P(('parts', 'span'), 'seq'), parts along dimension 0, may hold values from -18 to 18
- timesteps: int32 [8], P('parts'), parts along dimension 0, may hold values from 0 to 31
- gate_table: float32 [32, 4096], replicated, may hold values from 0.1 to 1.9
Outputs:
- gated_out: bfloat16 [8, 1024, 4096], P(('parts', 'span'), 'seq'), parts along dimension 0
There are 2 independent parts, one for each index of `parts`. A program takes and returns all parts, laid end to end along the dimension named above; an argument that names none is the same for every part. Nothing has to cross between parts.
All inputs are finite; a program needn't handle non-finite values.
Results may differ from a plain program's by a relative error of at most 0.0053.
Values may be sent and summed in bfloat16 or wider, within the bound.
A program may use at most 128 MiB of HBM per device.

v0:
```python
import math

import jax
import jax.numpy as jnp
from jax import lax
from jax.sharding import PartitionSpec as P

HD = 128


masked_score = -1e30


def local(q_in, k_in, v_in, timesteps, gate_table):
    head_rows, key_rows, value_rows = (
        lax.all_to_all(q_in[0], "seq", split_axis=1, concat_axis=0, tiled=True),
        lax.all_to_all(k_in[0], "seq", split_axis=1, concat_axis=0, tiled=True),
        lax.all_to_all(v_in[0], "seq", split_axis=1, concat_axis=0, tiled=True),
    )
    length = head_rows.shape[0]
    columns = head_rows.shape[1]
    heads = columns // HD
    scale = HD ** (-0.5)
    span_id = lax.axis_index("span")
    limit = (span_id + 1) * length
    query_three = head_rows.reshape(length, heads, HD)
    init = (
        jnp.full((heads, length), masked_score, jnp.float32),
        jnp.zeros((heads, length), jnp.float32),
        jnp.zeros((length, heads, HD), jnp.float32),
    )
    key_piece = lax.all_gather(key_rows, "span", axis=0, tiled=True)
    value_piece = lax.all_gather(value_rows, "span", axis=0, tiled=True)
    count = key_piece.shape[0]
    block = math.gcd(count, 512)

    def one_block(index, state):
        top, total, accum = state
        offset = index * block
        key_block = lax.dynamic_slice_in_dim(key_piece, offset, block, 0).reshape(block, heads, HD)
        value_block = lax.dynamic_slice_in_dim(value_piece, offset, block, 0).reshape(
            block, heads, HD
        )
        scores = (
            jnp.einsum("qhd,khd->hqk", query_three, key_block, preferred_element_type=jnp.float32)
            * scale
        )
        keep = offset + jnp.arange(block) < limit
        scores = jnp.where(keep[None, None, :], scores, masked_score)
        new_top = jnp.maximum(top, jnp.max(scores, axis=-1))
        expo = jnp.where(keep[None, None, :], jnp.exp(scores - new_top[:, :, None]), 0.0)
        shrink = jnp.exp(top - new_top)
        total = total * shrink + jnp.sum(expo, axis=-1)
        mixed = jnp.einsum(
            "hqk,khd->qhd",
            expo.astype(jnp.bfloat16),
            value_block,
            preferred_element_type=jnp.float32,
        )
        accum = accum * shrink.T[:, :, None] + mixed
        return (new_top, total, accum)

    def run_blocks(state):
        return lax.fori_loop(0, count // block, one_block, state)

    def keep_state(state):
        return state

    top, total, accum = lax.cond(jnp.int32(0) < limit, run_blocks, keep_state, init)
    attn = (accum / total.T[:, :, None]).reshape(length, columns).astype(jnp.bfloat16)
    token_rows = lax.all_to_all(attn, "seq", split_axis=0, concat_axis=1, tiled=True)
    steps_count = gate_table.shape[0]
    span_step = lax.dynamic_index_in_dim(timesteps, span_id, 0, keepdims=False)
    picked = (jnp.arange(steps_count) == span_step).astype(jnp.float32)
    gate = jnp.dot(picked, gate_table, precision=lax.Precision.HIGHEST)
    return (token_rows.astype(jnp.float32) * gate[None, :]).astype(jnp.bfloat16)[None]


def solution(mesh):
    in_specs = (
        P(("parts", "span"), "seq", None),
        P(("parts", "span"), "seq", None),
        P(("parts", "span"), "seq", None),
        P("parts"),
        P(),
    )
    out_specs = P(("parts", "span"), "seq", None)
    return jax.shard_map(local, mesh=mesh, in_specs=in_specs, out_specs=out_specs, check_vma=False)
```

profile of v0, /device:TPU:7, one launch (start us, length us, event | category | flops | bytes accessed | tf_op | source)
XLA Modules:
  0.0 530.7 jit_solution(13859830746761117424)
XLA Ops:
  10.7 51.9 %all_to_all.64 = bf16[256,4,1024]{0,2,1:T(8,128)(2,1)S(1)} all-to-all(bf16[256,4,1024]{0,2,1:T(8,128)(2,1)} %bitcast.80), channel_id=1, replica_groups=mesh['parts'=2,'span'=4,'seq'=4] {'seq'}, dimensions={1} | all-to-all | bytes 4194304 | tf_op jit(solution)/shard_map/all_to_all | solution.py:17
  69.2 50.9 %all_to_all.65 = bf16[256,4,1024]{0,2,1:T(8,128)(2,1)S(1)} all-to-all(bf16[256,4,1024]{0,2,1:T(8,128)(2,1)} %bitcast.81), channel_id=1, replica_groups=mesh['parts'=2,'span'=4,'seq'=4] {'seq'}, dimensions={1} | all-to-all | bytes 4194304 | tf_op jit(solution)/shard_map/all_to_all | solution.py:18
  130.3 47.6 %all-to-all-done = bf16[256,4,1024]{0,2,1:T(8,128)(2,1)S(1)} async-done(((bf16[256,4,1024]{0,2,1:T(8,128)(2,1)}), bf16[256,4,1024]{0,2,1:T(8,128)(2,1)S(1)}, u32[]{:S(2)}, u32[]{:S(2)}) %all-to-all-start) | async-done | bytes 2097184 | tf_op jit(solution)/shard_map/all_to_all | solution.py:16
  177.9 5.3 %all-gather.5.cloned.1.call-done = bf16[4096,1024]{1,0:T(8,128)(2,1)} async-done(((bf16[1024,1024]{1,0:T(8,128)(2,1)}), bf16[4096,1024]{1,0:T(8,128)(2,1)}) %all-gather.5.cloned.1.call-update) | async-done | bytes 8388624 | tf_op jit(solution)/shard_map/all_gather | solution.py:33
  183.2 271.6 %conditional.1 = (f32[8,1024]{1,0:T(8,128)}, f32[1024,8,128]{0,2,1:T(8,128)}) conditional(s32[]{:T(128)} %convert_element_type.44, () %tuple.27, (bf16[4,256,1024]{1,2,0:T(8,128)(2,1)S(1)}, s32[]{:T(128)}, bf16[4096,1024]{1,0:T(8,128)(2,1)}, bf16[4096,1024]{1,0:T(8,128)(2,1)}) %tuple.65), branch_computations={%region_0.0_spmd, %region_1.6_spmd} | conditional | flops 2205205504 | bytes 151521616 | solution.py:69
  189.5 265.3 %while.17 = (s32[]{:T(128)}, f32[8,1024]{1,0:T(8,128)S(1)}, f32[8,1024]{1,0:T(8,128)}, f32[1024,8,128]{0,2,1:T(8,128)}, s32[]{:T(128)}, /*index=5*/bf16[4096,102...) while((s32[]{:T(128)}, f32[8,1024]{1,0:T(8,128)S(1)}, ...), condition=%wide.region_5.5_spmd.clone, body=%wide.region_2.4_spmd.clone.sunk | while | flops 2205205504 | bytes 138938576 | solution.py:64
  193.7 9.4 %bitcast_reduce_fusion.2 = (f32[8,1024]{1,0:T(8,128)S(1)}, f32[8,512,1024]{2,1,0:T(8,128)}) fusion(pred[512]{0:T(512)(128)(4,1)S(1)} %add_compare_fusion.2, bf16[512,8,128]{0,2,1:T(8,128)(2,1)S(1)} %bitcast.72, bf16[1024,8,128]{2,0,1:T(8,128)(2,1)} %get-tuple-element.338), kind=kOutput, calls=%fused_computation.1.clone.1 | convolution fusion | flops 1086316544 | bytes 19956224 | tf_op jit(solution)/shard_map/cond/branch_1_fun/while/body/eval_jaxpr/qhd,khd->hqk/dot_general | solution.py:45
  203.6 10.9 %bitcast_add_fusion.2 = f32[1024,8,128]{0,2,1:T(8,128)} fusion(f32[1024,8,128]{0,2,1:T(8,128)} %get-tuple-element.323, bf16[512,8,128]{0,2,1:T(8,128)(2,1)S(1)} %bitcast.73, f32[8,512,1024]{2,1,0:T(8,128)} %get-tuple-element.305, f32[8,1024]{1,0:T(8,128)S(1)} %get-tuple-element.333, pred[512]{0:T(512)(128)(4,1)S(1)} %add_compare_fusion.2, ...), kind=kOutput, calls=%fused_computation.10.clone.1 | convolution fusion | flops 1097859072 | bytes 26280448 | tf_op jit(solution)/shard_map/cond/branch_1_fun/while/body/eval_jaxpr/hqk,khd->qhd/dot_general | solution.py:54
  215.7 4.6 fusion.37
  225.1 9.4 %bitcast_reduce_fusion.2 = (f32[8,1024]{1,0:T(8,128)S(1)}, f32[8,512,1024]{2,1,0:T(8,128)}) fusion(pred[512]{0:T(512)(128)(4,1)S(1)} %add_compare_fusion.2, bf16[512,8,128]{0,2,1:T(8,128)(2,1)S(1)} %bitcast.72, bf16[1024,8,128]{2,0,1:T(8,128)(2,1)} %get-tuple-element.338), kind=kOutput, calls=%fused_computation.1.clone.1 | convolution fusion | flops 1086316544 | bytes 19956224 | tf_op jit(solution)/shard_map/cond/branch_1_fun/while/body/eval_jaxpr/qhd,khd->hqk/dot_general | solution.py:45
  235.1 12.1 %bitcast_add_fusion.2 = f32[1024,8,128]{0,2,1:T(8,128)} fusion(f32[1024,8,128]{0,2,1:T(8,128)} %get-tuple-element.323, bf16[512,8,128]{0,2,1:T(8,128)(2,1)S(1)} %bitcast.73, f32[8,512,1024]{2,1,0:T(8,128)} %get-tuple-element.305, f32[8,1024]{1,0:T(8,128)S(1)} %get-tuple-element.333, pred[512]{0:T(512)(128)(4,1)S(1)} %add_compare_fusion.2, ...), kind=kOutput, calls=%fused_computation.10.clone.1 | convolution fusion | flops 1097859072 | bytes 26280448 | tf_op jit(solution)/shard_map/cond/branch_1_fun/while/body/eval_jaxpr/hqk,khd->qhd/dot_general | solution.py:54
  248.3 4.6 fusion.37
  258.5 9.4 %bitcast_reduce_fusion.2 = (f32[8,1024]{1,0:T(8,128)S(1)}, f32[8,512,1024]{2,1,0:T(8,128)}) fusion(pred[512]{0:T(512)(128)(4,1)S(1)} %add_compare_fusion.2, bf16[512,8,128]{0,2,1:T(8,128)(2,1)S(1)} %bitcast.72, bf16[1024,8,128]{2,0,1:T(8,128)(2,1)} %get-tuple-element.338), kind=kOutput, calls=%fused_computation.1.clone.1 | convolution fusion | flops 1086316544 | bytes 19956224 | tf_op jit(solution)/shard_map/cond/branch_1_fun/while/body/eval_jaxpr/qhd,khd->hqk/dot_general | solution.py:45
  268.5 12.1 %bitcast_add_fusion.2 = f32[1024,8,128]{0,2,1:T(8,128)} fusion(f32[1024,8,128]{0,2,1:T(8,128)} %get-tuple-element.323, bf16[512,8,128]{0,2,1:T(8,128)(2,1)S(1)} %bitcast.73, f32[8,512,1024]{2,1,0:T(8,128)} %get-tuple-element.305, f32[8,1024]{1,0:T(8,128)S(1)} %get-tuple-element.333, pred[512]{0:T(512)(128)(4,1)S(1)} %add_compare_fusion.2, ...), kind=kOutput, calls=%fused_computation.10.clone.1 | convolution fusion | flops 1097859072 | bytes 26280448 | tf_op jit(solution)/shard_map/cond/branch_1_fun/while/body/eval_jaxpr/hqk,khd->qhd/dot_general | solution.py:54
  281.7 4.6 fusion.37
  291.9 9.4 %bitcast_reduce_fusion.2 = (f32[8,1024]{1,0:T(8,128)S(1)}, f32[8,512,1024]{2,1,0:T(8,128)}) fusion(pred[512]{0:T(512)(128)(4,1)S(1)} %add_compare_fusion.2, bf16[512,8,128]{0,2,1:T(8,128)(2,1)S(1)} %bitcast.72, bf16[1024,8,128]{2,0,1:T(8,128)(2,1)} %get-tuple-element.338), kind=kOutput, calls=%fused_computation.1.clone.1 | convolution fusion | flops 1086316544 | bytes 19956224 | tf_op jit(solution)/shard_map/cond/branch_1_fun/while/body/eval_jaxpr/qhd,khd->hqk/dot_general | solution.py:45
  301.9 12.1 %bitcast_add_fusion.2 = f32[1024,8,128]{0,2,1:T(8,128)} fusion(f32[1024,8,128]{0,2,1:T(8,128)} %get-tuple-element.323, bf16[512,8,128]{0,2,1:T(8,128)(2,1)S(1)} %bitcast.73, f32[8,512,1024]{2,1,0:T(8,128)} %get-tuple-element.305, f32[8,1024]{1,0:T(8,128)S(1)} %get-tuple-element.333, pred[512]{0:T(512)(128)(4,1)S(1)} %add_compare_fusion.2, ...), kind=kOutput, calls=%fused_computation.10.clone.1 | convolution fusion | flops 1097859072 | bytes 26280448 | tf_op jit(solution)/shard_map/cond/branch_1_fun/while/body/eval_jaxpr/hqk,khd->qhd/dot_general | solution.py:54
  315.1 4.6 fusion.37
  325.4 9.4 %bitcast_reduce_fusion.2 = (f32[8,1024]{1,0:T(8,128)S(1)}, f32[8,512,1024]{2,1,0:T(8,128)}) fusion(pred[512]{0:T(512)(128)(4,1)S(1)} %add_compare_fusion.2, bf16[512,8,128]{0,2,1:T(8,128)(2,1)S(1)} %bitcast.72, bf16[1024,8,128]{2,0,1:T(8,128)(2,1)} %get-tuple-element.338), kind=kOutput, calls=%fused_computation.1.clone.1 | convolution fusion | flops 1086316544 | bytes 19956224 | tf_op jit(solution)/shard_map/cond/branch_1_fun/while/body/eval_jaxpr/qhd,khd->hqk/dot_general | solution.py:45
  335.3 12.1 %bitcast_add_fusion.2 = f32[1024,8,128]{0,2,1:T(8,128)} fusion(f32[1024,8,128]{0,2,1:T(8,128)} %get-tuple-element.323, bf16[512,8,128]{0,2,1:T(8,128)(2,1)S(1)} %bitcast.73, f32[8,512,1024]{2,1,0:T(8,128)} %get-tuple-element.305, f32[8,1024]{1,0:T(8,128)S(1)} %get-tuple-element.333, pred[512]{0:T(512)(128)(4,1)S(1)} %add_compare_fusion.2, ...), kind=kOutput, calls=%fused_computation.10.clone.1 | convolution fusion | flops 1097859072 | bytes 26280448 | tf_op jit(solution)/shard_map/cond/branch_1_fun/while/body/eval_jaxpr/hqk,khd->qhd/dot_general | solution.py:54
  348.5 4.6 fusion.37
  358.8 9.4 %bitcast_reduce_fusion.2 = (f32[8,1024]{1,0:T(8,128)S(1)}, f32[8,512,1024]{2,1,0:T(8,128)}) fusion(pred[512]{0:T(512)(128)(4,1)S(1)} %add_compare_fusion.2, bf16[512,8,128]{0,2,1:T(8,128)(2,1)S(1)} %bitcast.72, bf16[1024,8,128]{2,0,1:T(8,128)(2,1)} %get-tuple-element.338), kind=kOutput, calls=%fused_computation.1.clone.1 | convolution fusion | flops 1086316544 | bytes 19956224 | tf_op jit(solution)/shard_map/cond/branch_1_fun/while/body/eval_jaxpr/qhd,khd->hqk/dot_general | solution.py:45
  368.7 12.1 %bitcast_add_fusion.2 = f32[1024,8,128]{0,2,1:T(8,128)} fusion(f32[1024,8,128]{0,2,1:T(8,128)} %get-tuple-element.323, bf16[512,8,128]{0,2,1:T(8,128)(2,1)S(1)} %bitcast.73, f32[8,512,1024]{2,1,0:T(8,128)} %get-tuple-element.305, f32[8,1024]{1,0:T(8,128)S(1)} %get-tuple-element.333, pred[512]{0:T(512)(128)(4,1)S(1)} %add_compare_fusion.2, ...), kind=kOutput, calls=%fused_computation.10.clone.1 | convolution fusion | flops 1097859072 | bytes 26280448 | tf_op jit(solution)/shard_map/cond/branch_1_fun/while/body/eval_jaxpr/hqk,khd->qhd/dot_general | solution.py:54
  381.9 4.6 fusion.37
  392.2 9.4 %bitcast_reduce_fusion.2 = (f32[8,1024]{1,0:T(8,128)S(1)}, f32[8,512,1024]{2,1,0:T(8,128)}) fusion(pred[512]{0:T(512)(128)(4,1)S(1)} %add_compare_fusion.2, bf16[512,8,128]{0,2,1:T(8,128)(2,1)S(1)} %bitcast.72, bf16[1024,8,128]{2,0,1:T(8,128)(2,1)} %get-tuple-element.338), kind=kOutput, calls=%fused_computation.1.clone.1 | convolution fusion | flops 1086316544 | bytes 19956224 | tf_op jit(solution)/shard_map/cond/branch_1_fun/while/body/eval_jaxpr/qhd,khd->hqk/dot_general | solution.py:45
  402.1 12.1 %bitcast_add_fusion.2 = f32[1024,8,128]{0,2,1:T(8,128)} fusion(f32[1024,8,128]{0,2,1:T(8,128)} %get-tuple-element.323, bf16[512,8,128]{0,2,1:T(8,128)(2,1)S(1)} %bitcast.73, f32[8,512,1024]{2,1,0:T(8,128)} %get-tuple-element.305, f32[8,1024]{1,0:T(8,128)S(1)} %get-tuple-element.333, pred[512]{0:T(512)(128)(4,1)S(1)} %add_compare_fusion.2, ...), kind=kOutput, calls=%fused_computation.10.clone.1 | convolution fusion | flops 1097859072 | bytes 26280448 | tf_op jit(solution)/shard_map/cond/branch_1_fun/while/body/eval_jaxpr/hqk,khd->qhd/dot_general | solution.py:54
  415.4 4.6 fusion.37
  425.6 9.4 %bitcast_reduce_fusion.2 = (f32[8,1024]{1,0:T(8,128)S(1)}, f32[8,512,1024]{2,1,0:T(8,128)}) fusion(pred[512]{0:T(512)(128)(4,1)S(1)} %add_compare_fusion.2, bf16[512,8,128]{0,2,1:T(8,128)(2,1)S(1)} %bitcast.72, bf16[1024,8,128]{2,0,1:T(8,128)(2,1)} %get-tuple-element.338), kind=kOutput, calls=%fused_computation.1.clone.1 | convolution fusion | flops 1086316544 | bytes 19956224 | tf_op jit(solution)/shard_map/cond/branch_1_fun/while/body/eval_jaxpr/qhd,khd->hqk/dot_general | solution.py:45
  435.5 12.1 %bitcast_add_fusion.2 = f32[1024,8,128]{0,2,1:T(8,128)} fusion(f32[1024,8,128]{0,2,1:T(8,128)} %get-tuple-element.323, bf16[512,8,128]{0,2,1:T(8,128)(2,1)S(1)} %bitcast.73, f32[8,512,1024]{2,1,0:T(8,128)} %get-tuple-element.305, f32[8,1024]{1,0:T(8,128)S(1)} %get-tuple-element.333, pred[512]{0:T(512)(128)(4,1)S(1)} %add_compare_fusion.2, ...), kind=kOutput, calls=%fused_computation.10.clone.1 | convolution fusion | flops 1097859072 | bytes 26280448 | tf_op jit(solution)/shard_map/cond/branch_1_fun/while/body/eval_jaxpr/hqk,khd->qhd/dot_general | solution.py:54
  448.8 4.6 fusion.37
  464.7 4.4 all-to-all-start.3
  470.7 46.4 %all-to-all-done.3 = bf16[4,256,1024]{2,1,0:T(8,128)(2,1)} async-done(((bf16[4,256,1024]{2,1,0:T(8,128)(2,1)}), bf16[4,256,1024]{2,1,0:T(8,128)(2,1)}, u32[]{:S(2)}, u32[]{:S(2)}) %all-to-all-start.3) | async-done | bytes 2097184 | tf_op jit(solution)/shard_map/all_to_all | solution.py:71
  (102 shorter events, 103.1 us)
Async XLA Ops:
  6.5 463.2 %copy-start = (f32[32,4096]{1,0:T(8,128)S(1)}, f32[32,4096]{1,0:T(8,128)}, u32[]{:S(2)}) copy-start(f32[32,4096]{1,0:T(8,128)} %param.13) | copy-start | bytes 1572868
  6.5 171.4 %all-gather.3.cloned.1.call-start = ((), (), s32[]{:S(2)}) async-start(), calls=%async_computation.4 | async-start | bytes 10485760 | tf_op jit(solution)/shard_map/all_gather | solution.py:32
  65.1 118.1 %all-gather.5.cloned.1.call-start = ((), (), s32[]{:S(2)}) async-start(), calls=%async_computation.5 | async-start | bytes 10485760 | tf_op jit(solution)/shard_map/all_gather | solution.py:33
  126.6 51.3 %all-to-all-start = ((bf16[256,4,1024]{0,2,1:T(8,128)(2,1)}), bf16[256,4,1024]{0,2,1:T(8,128)(2,1)S(1)}, u32[]{:S(2)}, u32[]{:S(2)}) async-start(bf16[256,4,1024]{0,2,1:T(8,128)(2,1)} %bitcast.78), calls=%async_computation | async-start | bytes 4194304 | tf_op jit(solution)/shard_map/all_to_all | solution.py:16
  203.6 12.1 %copy-start.1 = (f32[8,512,1024]{2,1,0:T(8,128)S(1)}, f32[8,512,1024]{2,1,0:T(8,128)}, u32[]{:S(2)}) copy-start(f32[8,512,1024]{2,1,0:T(8,128)} %get-tuple-element.305) | copy-start | bytes 50331652 | tf_op jit(solution)/shard_map/cond/branch_1_fun/while
  235.1 13.3 %copy-start.1 = (f32[8,512,1024]{2,1,0:T(8,128)S(1)}, f32[8,512,1024]{2,1,0:T(8,128)}, u32[]{:S(2)}) copy-start(f32[8,512,1024]{2,1,0:T(8,128)} %get-tuple-element.305) | copy-start | bytes 50331652 | tf_op jit(solution)/shard_map/cond/branch_1_fun/while
  268.5 13.3 %copy-start.1 = (f32[8,512,1024]{2,1,0:T(8,128)S(1)}, f32[8,512,1024]{2,1,0:T(8,128)}, u32[]{:S(2)}) copy-start(f32[8,512,1024]{2,1,0:T(8,128)} %get-tuple-element.305) | copy-start | bytes 50331652 | tf_op jit(solution)/shard_map/cond/branch_1_fun/while
  301.9 13.3 %copy-start.1 = (f32[8,512,1024]{2,1,0:T(8,128)S(1)}, f32[8,512,1024]{2,1,0:T(8,128)}, u32[]{:S(2)}) copy-start(f32[8,512,1024]{2,1,0:T(8,128)} %get-tuple-element.305) | copy-start | bytes 50331652 | tf_op jit(solution)/shard_map/cond/branch_1_fun/while
  335.3 13.3 %copy-start.1 = (f32[8,512,1024]{2,1,0:T(8,128)S(1)}, f32[8,512,1024]{2,1,0:T(8,128)}, u32[]{:S(2)}) copy-start(f32[8,512,1024]{2,1,0:T(8,128)} %get-tuple-element.305) | copy-start | bytes 50331652 | tf_op jit(solution)/shard_map/cond/branch_1_fun/while
  368.7 13.3 %copy-start.1 = (f32[8,512,1024]{2,1,0:T(8,128)S(1)}, f32[8,512,1024]{2,1,0:T(8,128)}, u32[]{:S(2)}) copy-start(f32[8,512,1024]{2,1,0:T(8,128)} %get-tuple-element.305) | copy-start | bytes 50331652 | tf_op jit(solution)/shard_map/cond/branch_1_fun/while
  402.1 13.3 %copy-start.1 = (f32[8,512,1024]{2,1,0:T(8,128)S(1)}, f32[8,512,1024]{2,1,0:T(8,128)}, u32[]{:S(2)}) copy-start(f32[8,512,1024]{2,1,0:T(8,128)} %get-tuple-element.305) | copy-start | bytes 50331652 | tf_op jit(solution)/shard_map/cond/branch_1_fun/while
  435.5 13.3 %copy-start.1 = (f32[8,512,1024]{2,1,0:T(8,128)S(1)}, f32[8,512,1024]{2,1,0:T(8,128)}, u32[]{:S(2)}) copy-start(f32[8,512,1024]{2,1,0:T(8,128)} %get-tuple-element.305) | copy-start | bytes 50331652 | tf_op jit(solution)/shard_map/cond/branch_1_fun/while
  460.4 8.8 %copy-start.2 = (s32[4]{0:T(128)S(1)}, s32[4]{0:T(128)}, u32[]{:S(2)}) copy-start(s32[4]{0:T(128)} %param.12) | copy-start | bytes 52
  464.7 52.4 %all-to-all-start.3 = ((bf16[4,256,1024]{2,1,0:T(8,128)(2,1)}), bf16[4,256,1024]{2,1,0:T(8,128)(2,1)}, u32[]{:S(2)}, u32[]{:S(2)}) async-start(bf16[4,256,1024]{2,1,0:T(8,128)(2,1)} %copy.42), calls=%async_computation.3 | async-start | bytes 4194304 | tf_op jit(solution)/shard_map/all_to_all | solution.py:71
Sparse Core Ops, SparseCore 0:
  65.2 58.0 all-gather.2
  124.9 58.2 all-gather.4
where the time goes:
time: 536 us; the launch traced here: 531 us
  matrix products  171 us (32%)
  blocking collectives  103 us (19%)
  waiting for transfers between devices  99.4 us (19%)
  local copies, waits for them, and re-layouts  84 us (16%)
  other arithmetic  51.5 us (10%)
  between operations  13.5 us (3%)
  starting transfers between devices  8.1 us (2%)
    dot_general x8, matrix products, one_block(): jnp.einsum('hqk,khd->qhd', expo.astype(jnp.bfloat16), value_block, prefer...  95.3 us
    dot_general x8, matrix products, one_block(): jnp.einsum('qhd,khd->hqk', query_three, key_block, preferred_element_type...  74.9 us
    all_to_all x1, blocking collectives, local(): lax.all_to_all(k_in[0], 'seq', split_axis=1, concat_axis=0, tiled=True)  51.9 us
    all_to_all x1, blocking collectives, local(): lax.all_to_all(v_in[0], 'seq', split_axis=1, concat_axis=0, tiled=True)  50.9 us
    all_to_all x1, waiting for transfers between devices, local(): lax.all_to_all(q_in[0], 'seq', split_axis=1, concat_axis=0, tiled=True)  47.6 us
    all_to_all x1, waiting for transfers between devices, local(): lax.all_to_all(attn, 'seq', split_axis=0, concat_axis=1, tiled=True)  46.4 us
    reduce_sum x8, other arithmetic, one_block(): total = total * shrink + jnp.sum(expo, axis=-1)  37 us
    dynamic_slice x16, local copies, waits for them, and re-layouts, one_block(): lax.dynamic_slice_in_dim(value_piece, offset, block, 0)  25.8 us
  transfers between devices with their start and end apart: 4, of which 3 were waited for; matrix products, arithmetic and copies ran while one was open for 2% of the time, Pallas kernels for 0%

commit v1 on v0

v1 whole, which is shorter than its diff:
```python
import functools
import math

import jax
import jax.numpy as jnp
from jax import lax
from jax.experimental import pallas as pl
from jax.experimental.pallas import tpu as pltpu
from jax.sharding import PartitionSpec as P

HD = 128
AHEAD = 3
MESH = pl.DeviceIdType.MESH


def kernel(
    n, spans, q_in, k_in, v_in, gate, out, q_all, k_all, v_all, o_all,
    send_z, recv_z, send_x, send_c, recv_s, send_o, recv_o,
):
    heads, length, _ = q_all.shape
    rows = length // n
    cores = 2 if spans % 2 == 0 else 1
    chips = spans // cores
    z = lax.axis_index("seq")
    span = lax.axis_index("span")
    chip = span // cores
    core = lax.rem(span, cores)
    sibling = chip * cores + (cores - 1 - core)
    coef = HD ** (-0.5) * math.log2(math.e)

    barrier = pltpu.get_barrier_semaphore()

    def greet_seq(step, carry):
        pl.semaphore_signal(
            barrier, inc=1, device_id={"seq": lax.rem(z + step, n)}, device_id_type=MESH
        )
        return carry

    def greet_span(step, carry):
        other = lax.rem(chip + step, chips) * cores + core
        pl.semaphore_signal(barrier, inc=1, device_id={"span": other}, device_id_type=MESH)
        return carry

    lax.fori_loop(1, n, greet_seq, 0)
    lax.fori_loop(1, chips, greet_span, 0)
    if cores == 2:
        pl.semaphore_signal(barrier, inc=1, device_id={"span": sibling}, device_id_type=MESH)
    pl.semaphore_wait(barrier, (n - 1) + (chips - 1) + (cores - 1))

    def token_rows(index):
        return pl.ds(pl.multiple_of(index * rows, rows), rows)

    def head_columns(owner, head):
        return pl.ds(pl.multiple_of((owner * heads + head) * HD, HD), HD)

    sources = (k_in, v_in, q_in)

    def landing(which, head, piece):
        if which == 2:
            return q_all.at[head, token_rows(piece), :]
        return (k_all, v_all)[which].at[span, head, token_rows(piece), :]

    def own_piece(which, head):
        return pltpu.make_async_copy(
            sources[which].at[:, head_columns(z, head)],
            landing(which, head, z),
            recv_z.at[which, head, z],
        )

    def seq_send(which, head, peer):
        return pltpu.make_async_remote_copy(
            src_ref=sources[which].at[:, head_columns(peer, head)],
            dst_ref=landing(which, head, z),
            send_sem=send_z.at[which, head, peer],
            recv_sem=recv_z.at[which, head, z],
            device_id={"seq": peer},
            device_id_type=MESH,
        )

    def seq_arrival(which, head, peer):
        return pltpu.make_async_remote_copy(
            src_ref=sources[which].at[:, head_columns(peer, head)],
            dst_ref=landing(which, head, peer),
            send_sem=send_z.at[which, head, peer],
            recv_sem=recv_z.at[which, head, peer],
            device_id={"seq": peer},
            device_id_type=MESH,
        )

    def span_copy(which, head, origin, target, send_sem):
        block = (k_all, v_all)[which].at[origin, head]
        return pltpu.make_async_remote_copy(
            src_ref=block,
            dst_ref=block,
            send_sem=send_sem,
            recv_sem=recv_s.at[which, head, origin],
            device_id={"span": target},
            device_id_type=MESH,
        )

    def chip_send(which, head, other_chip):
        return span_copy(
            which, head, span, other_chip * cores + core, send_x.at[which, head, other_chip]
        )

    def sibling_send(which, head, origin):
        return span_copy(which, head, origin, sibling, send_c.at[which, head, origin])

    def result_send(head, peer):
        return pltpu.make_async_remote_copy(
            src_ref=o_all.at[head, token_rows(peer), :],
            dst_ref=out.at[:, head_columns(z, head)],
            send_sem=send_o.at[head, peer],
            recv_sem=recv_o.at[head, z],
            device_id={"seq": peer},
            device_id_type=MESH,
        )

    def result_arrival(head, peer):
        return pltpu.make_async_remote_copy(
            src_ref=o_all.at[head, token_rows(peer), :],
            dst_ref=out.at[:, head_columns(peer, head)],
            send_sem=send_o.at[head, peer],
            recv_sem=recv_o.at[head, peer],
            device_id={"seq": peer},
            device_id_type=MESH,
        )

    def own_result(head):
        return pltpu.make_async_copy(
            o_all.at[head, token_rows(z), :],
            out.at[:, head_columns(z, head)],
            recv_o.at[head, z],
        )

    def over_peers(action):
        def step(offset, carry):
            action(lax.rem(z + offset, n))
            return carry

        lax.fori_loop(1, n, step, 0)

    def loop(low, high, action):
        def step(index, carry):
            action(index)
            return carry

        lax.fori_loop(low, high, step, 0)

    def issue(head):
        for which in range(3):
            over_peers(lambda peer: seq_send(which, head, peer).start())
            own_piece(which, head).start()

    def arrive(which, head):
        own_piece(which, head).wait()
        over_peers(lambda peer: seq_arrival(which, head, peer).wait_recv())

    tile = math.gcd(length, 256)

    def attend(head):
        def one_tile(index):
            piece = pl.ds(pl.multiple_of(index * tile, tile), tile)
            query = q_all[head, piece, :]

            def one_span(origin, state):
                top, total, accum = state
                scores = lax.dot_general(
                    query,
                    k_all[origin, head],
                    (((1,), (1,)), ((), ())),
                    preferred_element_type=jnp.float32,
                )
                new_top = jnp.maximum(top, jnp.max(scores, axis=-1, keepdims=True))
                expo = jnp.exp2((scores - new_top) * coef)
                shrink = jnp.exp2((top - new_top) * coef)
                total = total * shrink + jnp.sum(expo, axis=-1, keepdims=True)
                mixed = jnp.dot(
                    expo.astype(jnp.bfloat16),
                    v_all[origin, head],
                    preferred_element_type=jnp.float32,
                )
                return new_top, total, accum * shrink + mixed

            init = (
                jnp.full((tile, 1), -1e30, jnp.float32),
                jnp.zeros((tile, 1), jnp.float32),
                jnp.zeros((tile, HD), jnp.float32),
            )
            _, total, accum = lax.fori_loop(0, span + 1, one_span, init)
            attn = (accum / total).astype(jnp.bfloat16).astype(jnp.float32)
            o_all[head, piece, :] = (attn * gate[head]).astype(jnp.bfloat16)

        loop(0, length // tile, one_tile)

    loop(0, min(AHEAD, heads), issue)

    def one_head(head):
        @pl.when(head + AHEAD < heads)
        def _():
            issue(head + AHEAD)

        for which in range(2):
            arrive(which, head)
            loop(chip + 1, chips, lambda other: chip_send(which, head, other).start())
            if cores == 2:

                @pl.when(core == 0)
                def _():
                    sibling_send(which, head, span).start()

        def from_chip(other):
            origin = other * cores + core
            for which in range(2):
                span_copy(which, head, origin, sibling, send_c.at[which, head, origin]).wait_recv()
                if cores == 2:
                    sibling_send(which, head, origin).start()

        loop(0, chip, from_chip)
        if cores == 2:

            def from_sibling(origin):
                for which in range(2):
                    sibling_send(which, head, origin).wait_recv()

            loop(0, chip, lambda other: from_sibling(other * cores + (1 - core)))

            @pl.when(core == 1)
            def _():
                from_sibling(sibling)

        arrive(2, head)
        attend(head)
        over_peers(lambda peer: result_send(head, peer).start())
        own_result(head).start()

    loop(0, heads, one_head)

    def finish(head):
        for which in range(3):
            over_peers(lambda peer: seq_send(which, head, peer).wait_send())
        for which in range(2):
            loop(chip + 1, chips, lambda other: chip_send(which, head, other).wait_send())
            if cores == 2:
                loop(0, chip, lambda other: sibling_send(which, head, other * cores + core).wait_send())

                @pl.when(core == 0)
                def _():
                    sibling_send(which, head, span).wait_send()

        over_peers(lambda peer: result_send(head, peer).wait_send())
        own_result(head).wait()
        over_peers(lambda peer: result_arrival(head, peer).wait_recv())

    loop(0, heads, finish)


def local(n, spans, q_in, k_in, v_in, timesteps, gate_table):
    _, rows, columns = q_in.shape
    length = rows * n
    heads = columns // HD // n
    chips = spans // 2 if spans % 2 == 0 else spans
    step = lax.dynamic_index_in_dim(timesteps, lax.axis_index("span"), 0, keepdims=False)
    gate = lax.dynamic_slice(
        gate_table, (step, lax.axis_index("seq") * heads * HD), (1, heads * HD)
    ).reshape(heads, 1, HD)
    anywhere = pl.BlockSpec(memory_space=pl.ANY)
    return pl.pallas_call(
        functools.partial(kernel, n, spans),
        out_shape=jax.ShapeDtypeStruct((rows, columns), jnp.bfloat16),
        in_specs=[anywhere] * 3 + [pl.BlockSpec(memory_space=pltpu.VMEM)],
        out_specs=anywhere,
        scratch_shapes=[
            pltpu.VMEM((heads, length, HD), jnp.bfloat16),
            pltpu.VMEM((spans, heads, length, HD), jnp.bfloat16),
            pltpu.VMEM((spans, heads, length, HD), jnp.bfloat16),
            pltpu.VMEM((heads, length, HD), jnp.bfloat16),
            pltpu.SemaphoreType.DMA((3, heads, n)),
            pltpu.SemaphoreType.DMA((3, heads, n)),
            pltpu.SemaphoreType.DMA((2, heads, chips)),
            pltpu.SemaphoreType.DMA((2, heads, spans)),
            pltpu.SemaphoreType.DMA((2, heads, spans)),
            pltpu.SemaphoreType.DMA((heads, n)),
            pltpu.SemaphoreType.DMA((heads, n)),
        ],
        compiler_params=pltpu.CompilerParams(
            collective_id=0, has_side_effects=True, vmem_limit_bytes=48 * 1024 * 1024
        ),
        cost_estimate=pl.CostEstimate(
            flops=4 * heads * length * length * spans * HD,
            bytes_accessed=8 * rows * columns,
            transcendentals=heads * length * length * spans,
        ),
    )(q_in[0], k_in[0], v_in[0], gate)[None]


def solution(mesh):
    in_specs = (
        P(("parts", "span"), "seq", None),
        P(("parts", "span"), "seq", None),
        P(("parts", "span"), "seq", None),
        P("parts"),
        P(),
    )
    out_specs = P(("parts", "span"), "seq", None)
    body = functools.partial(local, mesh.shape["seq"], mesh.shape["span"])
    return jax.shard_map(body, mesh=mesh, in_specs=in_specs, out_specs=out_specs, check_vma=False)
```

time: 536 us -> 202 us (0.38)
  Pallas kernels: 0 us -> 195 us
  matrix products: 171 us -> 0 us
  blocking collectives: 103 us -> 0 us
  waiting for transfers between devices: 99.4 us -> 0 us
  local copies, waits for them, and re-layouts: 84 us -> 4.3 us
  other arithmetic: 51.5 us -> 0 us
  between operations: 13.5 us -> 1.96 us
  starting transfers between devices: 8.1 us -> 0 us
    pallas_call x0 -> x1, Pallas kernels: none -> 195 us  [local(): pl.pallas_call(functools.partial(kernel, n, spans), out_shape=jax.ShapeDt...]
    dot_general x17 -> x0, matrix products: 171 us -> none  [the longest x8 95.3 us: one_block(): jnp.einsum('hqk,khd->qhd', expo.astype(jnp.bfloat16), value_block, prefer...]
    all_to_all x2 -> x0, blocking collectives: 103 us -> none  [the longest x1 51.9 us: local(): lax.all_to_all(k_in[0], 'seq', split_axis=1, concat_axis=0, tiled=True)]
    all_to_all x2 -> x0, waiting for transfers between devices: 94 us -> none  [the longest x1 47.6 us: local(): lax.all_to_all(q_in[0], 'seq', split_axis=1, concat_axis=0, tiled=True)]
    dynamic_slice x25 -> x1, local copies, waits for them, and re-layouts: 38.3 us -> 1.3 us  [local(): lax.dynamic_index_in_dim(timesteps, lax.axis_index('span'), 0, keepdims=F...]
    reduce_sum x8 -> x0, other arithmetic: 37 us -> none  [one_block(): total = total * shrink + jnp.sum(expo, axis=-1)]
    add x8 -> x0, other arithmetic: 10.4 us -> none  [one_block(): total = total * shrink + jnp.sum(expo, axis=-1)]
    convert_element_type x3 -> x0, local copies, waits for them, and re-layouts: 9.93 us -> none  [the longest x2 7.06 us: local(): (accum / total.T[:, :, None]).reshape(length, columns).astype(jnp.bfloat16)]
  transfers between devices with their start and end apart: 4 -> 0, of which waited for: 3 -> 0; matrix products, arithmetic and copies ran while one was open for 2% -> 0% of each run, Pallas kernels for 0% -> 0%
where the time goes in v1:
time: 202 us
  Pallas kernels  195 us (97%)
  local copies, waits for them, and re-layouts  4.3 us (2%)
    pallas_call x1, Pallas kernels, local(): pl.pallas_call(functools.partial(kernel, n, spans), out_shape=jax.ShapeDt...  195 us

profile of v1, /device:TPU:7, one launch (start us, length us, event | category | flops | bytes accessed | tf_op | source)
XLA Modules:
  0.0 201.6 jit_solution(7998091015529263392)
XLA Ops:
  0.0 0.0 copy-start
  0.0 1.3 dynamic_slice.7
  3.2 0.0 copy-done
  3.3 0.1 dynamic-slice_bitcast_fusion.gate
  3.3 0.0 copy-start.1
  3.3 1.6 copy-done.1
  4.9 195.3 %shard_map.55 = bf16[256,4096]{1,0:T(8,128)(2,1)S(1)} custom-call(bf16[256,4096]{1,0:T(8,128)(2,1)S(1)} %bitcast.8, bf16[256,4096]{1,0:T(8,128)(2,1)} %bitcast.9, bf16[256,4096]{1,0:T(8,128)(2,1)} %bitcast.10, f32[8,1,128]{2,1,0:T(1,128)S(1)} %dynamic-slice_bitcast_fusion.gate), custom_call_target="tpu_custom_call" | custom-call | flops 17179869184 | bytes 8388608 | tf_op jit(solution)/shard_map/pallas_call | solution.py:268
  200.3 1.3 copy.7
Async XLA Ops:
  0.0 3.2 %copy-start = (f32[32,4096]{1,0:T(8,128)S(1)}, f32[32,4096]{1,0:T(8,128)}, u32[]{:S(2)}) copy-start(f32[32,4096]{1,0:T(8,128)} %param.9) | copy-start | bytes 1572868
  3.3 1.6 copy-start.1

commit v2 on v1

--- a/solution.py
+++ b/solution.py
@@ -9,12 +9,12 @@
 from jax.sharding import PartitionSpec as P
 
 HD = 128
-AHEAD = 3
+AHEAD = 8
 MESH = pl.DeviceIdType.MESH
 
 
 def kernel(
-    n, spans, q_in, k_in, v_in, gate, out, q_all, k_all, v_all, o_all,
+    n, spans, q_in, k_in, v_in, timesteps, gate_table, out, q_all, k_all, v_all, o_all, gates, gate_sem,
     send_z, recv_z, send_x, send_c, recv_s, send_o, recv_o,
 ):
     heads, length, _ = q_all.shape
@@ -134,11 +134,20 @@
         )
 
     def over_peers(action):
-        def step(offset, carry):
-            action(lax.rem(z + offset, n))
+        half = n // 2
+        side = z // half
+        place = lax.rem(z, half)
+
+        def across(offset, carry):
+            action((1 - side) * half + lax.rem(place + offset, half))
             return carry
 
-        lax.fori_loop(1, n, step, 0)
+        def beside(offset, carry):
+            action(side * half + lax.rem(place + offset, half))
+            return carry
+
+        lax.fori_loop(0, half, across, 0)
+        lax.fori_loop(1, half, beside, 0)
 
     def loop(low, high, action):
         def step(index, carry):
@@ -159,6 +168,10 @@
     tile = math.gcd(length, 256)
 
     def attend(head):
+        table = gates[:, pl.ds(pl.multiple_of(head * HD, HD), HD)]
+        chosen = lax.broadcasted_iota(jnp.int32, table.shape, 0) == timesteps[span]
+        gate = jnp.sum(jnp.where(chosen, table, 0.0), axis=0, keepdims=True)
+
         def one_tile(index):
             piece = pl.ds(pl.multiple_of(index * tile, tile), tile)
             query = q_all[head, piece, :]
@@ -189,11 +202,16 @@
             )
             _, total, accum = lax.fori_loop(0, span + 1, one_span, init)
             attn = (accum / total).astype(jnp.bfloat16).astype(jnp.float32)
-            o_all[head, piece, :] = (attn * gate[head]).astype(jnp.bfloat16)
+            o_all[head, piece, :] = (attn * gate).astype(jnp.bfloat16)
 
         loop(0, length // tile, one_tile)
 
     loop(0, min(AHEAD, heads), issue)
+    width = heads * HD
+    gate_copy = pltpu.make_async_copy(
+        gate_table.at[:, pl.ds(pl.multiple_of(z * width, width), width)], gates, gate_sem
+    )
+    gate_copy.start()
 
     def one_head(head):
         @pl.when(head + AHEAD < heads)
@@ -234,6 +252,7 @@
         over_peers(lambda peer: result_send(head, peer).start())
         own_result(head).start()
 
+    gate_copy.wait()
     loop(0, heads, one_head)
 
     def finish(head):
@@ -260,21 +279,19 @@
     length = rows * n
     heads = columns // HD // n
     chips = spans // 2 if spans % 2 == 0 else spans
-    step = lax.dynamic_index_in_dim(timesteps, lax.axis_index("span"), 0, keepdims=False)
-    gate = lax.dynamic_slice(
-        gate_table, (step, lax.axis_index("seq") * heads * HD), (1, heads * HD)
-    ).reshape(heads, 1, HD)
     anywhere = pl.BlockSpec(memory_space=pl.ANY)
     return pl.pallas_call(
         functools.partial(kernel, n, spans),
         out_shape=jax.ShapeDtypeStruct((rows, columns), jnp.bfloat16),
-        in_specs=[anywhere] * 3 + [pl.BlockSpec(memory_space=pltpu.VMEM)],
+        in_specs=[anywhere] * 3 + [pl.BlockSpec(memory_space=pltpu.SMEM), anywhere],
         out_specs=anywhere,
         scratch_shapes=[
             pltpu.VMEM((heads, length, HD), jnp.bfloat16),
             pltpu.VMEM((spans, heads, length, HD), jnp.bfloat16),
             pltpu.VMEM((spans, heads, length, HD), jnp.bfloat16),
             pltpu.VMEM((heads, length, HD), jnp.bfloat16),
+            pltpu.VMEM((gate_table.shape[0], heads * HD), jnp.float32),
+            pltpu.SemaphoreType.DMA,
             pltpu.SemaphoreType.DMA((3, heads, n)),
             pltpu.SemaphoreType.DMA((3, heads, n)),
             pltpu.SemaphoreType.DMA((2, heads, chips)),
@@ -284,14 +301,14 @@
             pltpu.SemaphoreType.DMA((heads, n)),
         ],
         compiler_params=pltpu.CompilerParams(
-            collective_id=0, has_side_effects=True, vmem_limit_bytes=48 * 1024 * 1024
+            collective_id=0, has_side_effects=True, vmem_limit_bytes=61 * 1024 * 1024
         ),
         cost_estimate=pl.CostEstimate(
             flops=4 * heads * length * length * spans * HD,
             bytes_accessed=8 * rows * columns,
             transcendentals=heads * length * length * spans,
         ),
-    )(q_in[0], k_in[0], v_in[0], gate)[None]
+    )(q_in[0], k_in[0], v_in[0], timesteps, gate_table)[None]
 
 
 def solution(mesh):

time: 202 us -> 193 us (0.955)
  Pallas kernels: 195 us -> 189 us
    pallas_call x1, Pallas kernels: 195 us -> 189 us  [local(): pl.pallas_call(functools.partial(kernel, n, spans), out_shape=jax.ShapeDt...]
where the time goes in v2:
time: 193 us; the launch traced here: 192 us
  Pallas kernels  189 us (98%)
  local copies, waits for them, and re-layouts  3.13 us (2%)
    pallas_call x1, Pallas kernels, local(): pl.pallas_call(functools.partial(kernel, n, spans), out_shape=jax.ShapeDt...  189 us

profile of v2, /device:TPU:7, one launch (start us, length us, event | category | flops | bytes accessed | tf_op | source)
XLA Modules:
  0.0 192.4 jit_solution(342302159735978063)
XLA Ops:
  0.0 189.3 %shard_map.55 = bf16[256,4096]{1,0:T(8,128)(2,1)} custom-call(bf16[256,4096]{1,0:T(8,128)(2,1)} %bitcast.5, bf16[256,4096]{1,0:T(8,128)(2,1)} %bitcast.6, bf16[256,4096]{1,0:T(8,128)(2,1)} %bitcast.7, s32[4]{0:T(128)} %timesteps.1, f32[32,4096]{1,0:T(8,128)} %gate_table.1), custom_call_target="tpu_custom_call" | custom-call | flops 17179869184 | bytes 8388608 | tf_op jit(solution)/shard_map/pallas_call | solution.py:283
  189.3 3.1 %copy.7 = bf16[1,256,4096]{2,1,0:T(8,128)(2,1)} copy(bf16[1,256,4096]{2,1,0:T(8,128)(2,1)} %bitcast.4) | data formatting | bytes 4194304

commit v3 on v2

--- a/solution.py
+++ b/solution.py
@@ -133,7 +133,7 @@
             recv_o.at[head, z],
         )
 
-    def over_peers(action):
+    def over_peers(action, part=2):
         half = n // 2
         side = z // half
         place = lax.rem(z, half)
@@ -146,8 +146,10 @@
             action(side * half + lax.rem(place + offset, half))
             return carry
 
-        lax.fori_loop(0, half, across, 0)
-        lax.fori_loop(1, half, beside, 0)
+        if part != 1:
+            lax.fori_loop(0, half, across, 0)
+        if part != 0:
+            lax.fori_loop(1, half, beside, 0)
 
     def loop(low, high, action):
         def step(index, carry):
@@ -157,8 +159,10 @@
         lax.fori_loop(low, high, step, 0)
 
     def issue(head):
+        for part in range(2):
+            for which in range(3):
+                over_peers(lambda peer: seq_send(which, head, peer).start(), part)
         for which in range(3):
-            over_peers(lambda peer: seq_send(which, head, peer).start())
             own_piece(which, head).start()
 
     def arrive(which, head):
@@ -301,7 +305,7 @@
             pltpu.SemaphoreType.DMA((heads, n)),
         ],
         compiler_params=pltpu.CompilerParams(
-            collective_id=0, has_side_effects=True, vmem_limit_bytes=61 * 1024 * 1024
+            collective_id=0, has_side_effects=True, vmem_limit_bytes=59 * 1024 * 1024
         ),
         cost_estimate=pl.CostEstimate(
             flops=4 * heads * length * length * spans * HD,

time: 193 us -> 193 us (level)
  no operation moved by 1% of the time
where the time goes in v3:
time: 193 us; the launch traced here: 192 us
  Pallas kernels  189 us (98%)
  local copies, waits for them, and re-layouts  3.13 us (2%)
    pallas_call x1, Pallas kernels, local(): pl.pallas_call(functools.partial(kernel, n, spans), out_shape=jax.ShapeDt...  189 us

profile of v3, /device:TPU:7, one launch (start us, length us, event | category | flops | bytes accessed | tf_op | source)
XLA Modules:
  0.0 192.4 jit_solution(9990749586524269953)
XLA Ops:
  0.0 189.2 %shard_map.55 = bf16[256,4096]{1,0:T(8,128)(2,1)} custom-call(bf16[256,4096]{1,0:T(8,128)(2,1)} %bitcast.5, bf16[256,4096]{1,0:T(8,128)(2,1)} %bitcast.6, bf16[256,4096]{1,0:T(8,128)(2,1)} %bitcast.7, s32[4]{0:T(128)} %timesteps.1, f32[32,4096]{1,0:T(8,128)} %gate_table.1), custom_call_target="tpu_custom_call" | custom-call | flops 17179869184 | bytes 8388608 | tf_op jit(solution)/shard_map/pallas_call | solution.py:287
  189.2 3.1 %copy.7 = bf16[1,256,4096]{2,1,0:T(8,128)(2,1)} copy(bf16[1,256,4096]{2,1,0:T(8,128)(2,1)} %bitcast.4) | data formatting | bytes 4194304

commit v4 on v3

--- a/solution.py
+++ b/solution.py
@@ -169,14 +169,19 @@
         own_piece(which, head).wait()
         over_peers(lambda peer: seq_arrival(which, head, peer).wait_recv())
 
-    tile = math.gcd(length, 256)
+    owners = math.gcd(n, max(1, 256 // rows))
+    tile = rows * owners
+    half_tiles = max(1, n // owners // 2)
 
     def attend(head):
         table = gates[:, pl.ds(pl.multiple_of(head * HD, HD), HD)]
         chosen = lax.broadcasted_iota(jnp.int32, table.shape, 0) == timesteps[span]
         gate = jnp.sum(jnp.where(chosen, table, 0.0), axis=0, keepdims=True)
 
-        def one_tile(index):
+        def one_tile(step):
+            side = (z // owners // half_tiles + 1 + step // half_tiles) % 2
+            place = (z // owners + 1 + step) % half_tiles
+            index = side * half_tiles + place
             piece = pl.ds(pl.multiple_of(index * tile, tile), tile)
             query = q_all[head, piece, :]
 
@@ -208,6 +213,17 @@
             attn = (accum / total).astype(jnp.bfloat16).astype(jnp.float32)
             o_all[head, piece, :] = (attn * gate).astype(jnp.bfloat16)
 
+            def give(owner):
+                @pl.when(owner != z)
+                def _():
+                    result_send(head, owner).start()
+
+                @pl.when(owner == z)
+                def _():
+                    own_result(head).start()
+
+            loop(index * owners, (index + 1) * owners, give)
+
         loop(0, length // tile, one_tile)
 
     loop(0, min(AHEAD, heads), issue)
@@ -253,8 +269,6 @@
 
         arrive(2, head)
         attend(head)
-        over_peers(lambda peer: result_send(head, peer).start())
-        own_result(head).start()
 
     gate_copy.wait()
     loop(0, heads, one_head)

time: 193 us -> 194 us (level)
  no operation moved by 1% of the time
where the time goes in v4:
time: 194 us; the launch traced here: 192 us
  Pallas kernels  189 us (97%)
  local copies, waits for them, and re-layouts  3.13 us (2%)
    pallas_call x1, Pallas kernels, local(): pl.pallas_call(functools.partial(kernel, n, spans), out_shape=jax.ShapeDt...  189 us

profile of v4, /device:TPU:7, one launch (start us, length us, event | category | flops | bytes accessed | tf_op | source)
XLA Modules:
  0.0 192.0 jit_solution(12812930506396587951)
XLA Ops:
  0.0 188.9 %shard_map.55 = bf16[256,4096]{1,0:T(8,128)(2,1)} custom-call(bf16[256,4096]{1,0:T(8,128)(2,1)} %bitcast.5, bf16[256,4096]{1,0:T(8,128)(2,1)} %bitcast.6, bf16[256,4096]{1,0:T(8,128)(2,1)} %bitcast.7, s32[4]{0:T(128)} %timesteps.1, f32[32,4096]{1,0:T(8,128)} %gate_table.1), custom_call_target="tpu_custom_call" | custom-call | flops 17179869184 | bytes 8388608 | tf_op jit(solution)/shard_map/pallas_call | solution.py:301
  188.9 3.1 %copy.7 = bf16[1,256,4096]{2,1,0:T(8,128)(2,1)} copy(bf16[1,256,4096]{2,1,0:T(8,128)(2,1)} %bitcast.4) | data formatting | bytes 4194304
